TPU v7x, 256 devices: a whole 4x4x8 slice. The times are simulated.
256 devices in a mesh: ctx: 16 (over x_hi, z), head: 8 (over y, core), pair: 2 (over x_lo).
Axes of the slice: x: 4 (x_hi: 2, x_lo: 2; x = x_hi * 2 + x_lo), y: 4, z: 8, core: 2. Of those that a mesh axis runs over, the one named last changes fastest.
Arguments:
- queries: bfloat16 [2048, 64, 128], P(('pair', 'ctx'), 'head'), parts along dimension 0, may hold values from -6 to 6
- keys: bfloat16 [65536, 8, 128], P(('pair', 'ctx'), 'head'), parts along dimension 0, may hold values from -6 to 6
- values: bfloat16 [65536, 8, 128], P(('pair', 'ctx'), 'head'), parts along dimension 0, may hold values from -6 to 6
- lengths: int32 [4], P('pair'), parts along dimension 0, may hold values from 256 to 512, as said below
- prompt_lengths: int32 [2], P('pair'), parts along dimension 0, may hold values from 16384 to 32768
- out_weight: bfloat16 [8192, 8192], P('head', 'ctx'), may hold values from -0.0625 to 0.0625
Outputs:
- projected: float32 [2048, 8192], P(('pair', 'head'), 'ctx'), parts along dimension 0
There are 2 independent parts, one for each index of `pair`. A program takes and returns all parts, laid end to end along the dimension named above; an argument that names none is the same for every part. Nothing has to cross between parts.
Inputs may be any that keep to these rules, and one draw needn't show every extreme that they name: `lengths`: one of the two responses has exactly 512 real tokens, the other at least 256.
All inputs are finite; a program needn't handle non-finite values.
Results may differ from a plain program's by a relative error of at most 0.013.
Values may be sent and summed in bfloat16 or wider, within the bound.
A program may use at most 64 MiB of HBM per device.

v0:
```python
import jax
import jax.numpy as jnp
from jax import lax
from jax.sharding import PartitionSpec as P

RESP = 512


masked_score = -1e30


def shifted(value, axis, steps):
    count = lax.axis_size(axis)
    pairs = [(source, (source + steps) % count) for source in range(count)]
    return lax.ppermute(value, axis, pairs)


def block_terms(query_block, keys, values, key_start, prompt_lengths):
    query_rows, head_local, head_dim = query_block.shape
    key_rows, kv_local, _ = keys.shape
    group_size = head_local // kv_local
    grouped = query_block.reshape(query_rows, kv_local, group_size, head_dim)
    scores = jnp.einsum("qgjd,kgd->qgjk", grouped, keys, preferred_element_type=jnp.float32)
    scores = scores * head_dim ** (-0.5)
    key_pos = key_start + jnp.arange(key_rows, dtype=jnp.int32)
    visible = (key_pos < prompt_lengths[0])[None, None, None, :]
    scores = jnp.where(visible, scores, masked_score)
    peak = jnp.max(scores, axis=3)
    weights = jnp.where(visible, jnp.exp(scores - peak[..., None]), 0.0)
    total = jnp.sum(weights, axis=3)
    running = jnp.einsum(
        "qgjk,kgd->qgjd", weights.astype(jnp.bfloat16), values, preferred_element_type=jnp.float32
    )
    return (running, peak, total)


def combine(older, newer):
    overall = jnp.maximum(older[1], newer[1])
    old_factor = jnp.exp(older[1] - overall)
    new_factor = jnp.exp(newer[1] - overall)
    running = older[0] * old_factor[..., None] + newer[0] * new_factor[..., None]
    return (running, overall, older[2] * old_factor + newer[2] * new_factor)


def body(queries, keys, values, lengths, prompt_lengths, out_weight):
    cycle_size = lax.axis_size("ctx")
    position = lax.axis_index("ctx")
    query_rows, head_local, head_dim = queries.shape
    key_rows, kv_local, _ = keys.shape
    group_size = head_local // kv_local
    key_start = position * key_rows
    start_state = (
        queries,
        jnp.zeros((query_rows, kv_local, group_size, head_dim), jnp.float32),
        jnp.full((query_rows, kv_local, group_size), masked_score, jnp.float32),
        jnp.zeros((query_rows, kv_local, group_size), jnp.float32),
    )

    def turn(turn_index, carry):
        query_block = carry[0]
        fresh = block_terms(query_block, keys, values, key_start, prompt_lengths)
        running, peak, total = combine((carry[1], carry[2], carry[3]), fresh)
        query_block = shifted(query_block, "ctx", 1)
        running, peak, total = shifted((running, peak, total), "ctx", 1)
        return (query_block, running, peak, total)

    final_state = lax.fori_loop(0, cycle_size, turn, start_state)
    running, total = (final_state[1], final_state[3])
    row_ids = position * query_rows + jnp.arange(query_rows, dtype=jnp.int32)
    response_id = row_ids // RESP
    is_live = row_ids % RESP < jnp.where(response_id == 0, lengths[0], lengths[1])
    mixed = running / total[..., None]
    mixed = jnp.where(is_live[:, None, None, None], mixed, 0.0)
    mixed = mixed.reshape(query_rows, head_local * head_dim).astype(jnp.bfloat16)
    partial_sums = jnp.dot(
        lax.all_gather(mixed, "ctx", axis=0, tiled=True),
        out_weight,
        preferred_element_type=jnp.float32,
    )
    return lax.psum_scatter(partial_sums, "head", scatter_dimension=0, tiled=True)


def solution(mesh):
    in_specs = (
        P(("pair", "ctx"), "head", None),
        P(("pair", "ctx"), "head", None),
        P(("pair", "ctx"), "head", None),
        P("pair"),
        P("pair"),
        P("head", "ctx"),
    )
    out_specs = P(("pair", "head"), "ctx")
    return jax.shard_map(body, mesh=mesh, in_specs=in_specs, out_specs=out_specs, check_vma=False)
```

profile of v0, /device:TPU:7, one launch (start us, length us, event | category | flops | bytes accessed | tf_op | source)
XLA Modules:
  0.0 421.6 jit_solution(18025361927109579358)
XLA Ops:
  6.5 1.4 fusion.22
  8.9 271.0 %while.16 = (s32[]{:T(128)}, bf16[64,8,128]{2,0,1:T(8,128)(2,1)S(1)}, f32[64,1,8,128]{3,2,0,1:T(8,128)S(1)}, f32[64,1,8]{0,2,1:T(8,128)S(1)}, f32[64,1,8]{0,2,1:...) while((s32[]{:T(128)}, ...), condition=%wide.region_3.4_spmd, body=%wide.region_0.3_spmd.sunk | while | flops 550705152 | bytes 18805032 | solution.py:67
  9.6 1.9 bitcast_reduce_fusion.2
  11.6 1.1 fusion.38
  14.1 1.7 collective-permute-start.1
  15.8 1.6 collective-permute-start
  17.4 1.6 collective-permute-start.2
  19.1 2.8 collective-permute-start.3
  21.9 7.6 %collective-permute-done.2 = f32[64,1,8]{0,2,1:T(8,128)S(1)} collective-permute-done((f32[64,1,8]{0,2,1:T(8,128)S(1)}, f32[64,1,8]{0,2,1:T(8,128)S(1)}, u32[]{:S(2)}, u32[]{:S(2)}) %collective-permute-start.2) | collective-permute-done | bytes 2080 | tf_op jit(solution)/shard_map/while/body/eval_jaxpr/ppermute | solution.py:15
  30.3 1.9 bitcast_reduce_fusion.2
  32.2 1.1 fusion.38
  35.1 3.4 collective-permute-start.3
  38.5 9.4 %collective-permute-done.2 = f32[64,1,8]{0,2,1:T(8,128)S(1)} collective-permute-done((f32[64,1,8]{0,2,1:T(8,128)S(1)}, f32[64,1,8]{0,2,1:T(8,128)S(1)}, u32[]{:S(2)}, u32[]{:S(2)}) %collective-permute-start.2) | collective-permute-done | bytes 2080 | tf_op jit(solution)/shard_map/while/body/eval_jaxpr/ppermute | solution.py:15
  48.7 1.9 bitcast_reduce_fusion.2
  50.6 1.1 fusion.38
  51.7 1.0 fusion.37
  54.2 11.2 %collective-permute-done.2 = f32[64,1,8]{0,2,1:T(8,128)S(1)} collective-permute-done((f32[64,1,8]{0,2,1:T(8,128)S(1)}, f32[64,1,8]{0,2,1:T(8,128)S(1)}, u32[]{:S(2)}, u32[]{:S(2)}) %collective-permute-start.2) | collective-permute-done | bytes 2080 | tf_op jit(solution)/shard_map/while/body/eval_jaxpr/ppermute | solution.py:15
  66.1 1.9 bitcast_reduce_fusion.2
  68.1 1.1 fusion.38
  69.2 1.0 fusion.37
  71.0 10.9 %collective-permute-done.2 = f32[64,1,8]{0,2,1:T(8,128)S(1)} collective-permute-done((f32[64,1,8]{0,2,1:T(8,128)S(1)}, f32[64,1,8]{0,2,1:T(8,128)S(1)}, u32[]{:S(2)}, u32[]{:S(2)}) %collective-permute-start.2) | collective-permute-done | bytes 2080 | tf_op jit(solution)/shard_map/while/body/eval_jaxpr/ppermute | solution.py:15
  82.7 1.9 bitcast_reduce_fusion.2
  84.6 1.1 fusion.38
  87.5 10.0 %collective-permute-done.2 = f32[64,1,8]{0,2,1:T(8,128)S(1)} collective-permute-done((f32[64,1,8]{0,2,1:T(8,128)S(1)}, f32[64,1,8]{0,2,1:T(8,128)S(1)}, u32[]{:S(2)}, u32[]{:S(2)}) %collective-permute-start.2) | collective-permute-done | bytes 2080 | tf_op jit(solution)/shard_map/while/body/eval_jaxpr/ppermute | solution.py:15
  98.3 1.9 bitcast_reduce_fusion.2
  100.2 1.1 fusion.38
  103.1 10.0 %collective-permute-done.2 = f32[64,1,8]{0,2,1:T(8,128)S(1)} collective-permute-done((f32[64,1,8]{0,2,1:T(8,128)S(1)}, f32[64,1,8]{0,2,1:T(8,128)S(1)}, u32[]{:S(2)}, u32[]{:S(2)}) %collective-permute-start.2) | collective-permute-done | bytes 2080 | tf_op jit(solution)/shard_map/while/body/eval_jaxpr/ppermute | solution.py:15
  113.8 1.9 bitcast_reduce_fusion.2
  115.8 1.1 fusion.38
  116.9 1.0 fusion.37
  118.6 10.0 %collective-permute-done.2 = f32[64,1,8]{0,2,1:T(8,128)S(1)} collective-permute-done((f32[64,1,8]{0,2,1:T(8,128)S(1)}, f32[64,1,8]{0,2,1:T(8,128)S(1)}, u32[]{:S(2)}, u32[]{:S(2)}) %collective-permute-start.2) | collective-permute-done | bytes 2080 | tf_op jit(solution)/shard_map/while/body/eval_jaxpr/ppermute | solution.py:15
  129.4 1.9 bitcast_reduce_fusion.2
  131.3 1.1 fusion.38
  134.2 10.0 %collective-permute-done.2 = f32[64,1,8]{0,2,1:T(8,128)S(1)} collective-permute-done((f32[64,1,8]{0,2,1:T(8,128)S(1)}, f32[64,1,8]{0,2,1:T(8,128)S(1)}, u32[]{:S(2)}, u32[]{:S(2)}) %collective-permute-start.2) | collective-permute-done | bytes 2080 | tf_op jit(solution)/shard_map/while/body/eval_jaxpr/ppermute | solution.py:15
  144.9 1.9 bitcast_reduce_fusion.2
  146.9 1.1 fusion.38
  148.0 1.0 fusion.37
  149.8 10.0 %collective-permute-done.2 = f32[64,1,8]{0,2,1:T(8,128)S(1)} collective-permute-done((f32[64,1,8]{0,2,1:T(8,128)S(1)}, f32[64,1,8]{0,2,1:T(8,128)S(1)}, u32[]{:S(2)}, u32[]{:S(2)}) %collective-permute-start.2) | collective-permute-done | bytes 2080 | tf_op jit(solution)/shard_map/while/body/eval_jaxpr/ppermute | solution.py:15
  160.5 1.9 bitcast_reduce_fusion.2
  162.5 1.1 fusion.38
  165.3 10.0 %collective-permute-done.2 = f32[64,1,8]{0,2,1:T(8,128)S(1)} collective-permute-done((f32[64,1,8]{0,2,1:T(8,128)S(1)}, f32[64,1,8]{0,2,1:T(8,128)S(1)}, u32[]{:S(2)}, u32[]{:S(2)}) %collective-permute-start.2) | collective-permute-done | bytes 2080 | tf_op jit(solution)/shard_map/while/body/eval_jaxpr/ppermute | solution.py:15
  176.1 1.9 bitcast_reduce_fusion.2
  178.0 1.1 fusion.38
  179.1 1.0 fusion.37
  180.9 10.0 %collective-permute-done.2 = f32[64,1,8]{0,2,1:T(8,128)S(1)} collective-permute-done((f32[64,1,8]{0,2,1:T(8,128)S(1)}, f32[64,1,8]{0,2,1:T(8,128)S(1)}, u32[]{:S(2)}, u32[]{:S(2)}) %collective-permute-start.2) | collective-permute-done | bytes 2080 | tf_op jit(solution)/shard_map/while/body/eval_jaxpr/ppermute | solution.py:15
  191.6 1.9 bitcast_reduce_fusion.2
  193.6 1.1 fusion.38
  196.5 10.1 %collective-permute-done.2 = f32[64,1,8]{0,2,1:T(8,128)S(1)} collective-permute-done((f32[64,1,8]{0,2,1:T(8,128)S(1)}, f32[64,1,8]{0,2,1:T(8,128)S(1)}, u32[]{:S(2)}, u32[]{:S(2)}) %collective-permute-start.2) | collective-permute-done | bytes 2080 | tf_op jit(solution)/shard_map/while/body/eval_jaxpr/ppermute | solution.py:15
  207.3 1.9 bitcast_reduce_fusion.2
  209.2 1.1 fusion.38
  212.1 11.1 %collective-permute-done.2 = f32[64,1,8]{0,2,1:T(8,128)S(1)} collective-permute-done((f32[64,1,8]{0,2,1:T(8,128)S(1)}, f32[64,1,8]{0,2,1:T(8,128)S(1)}, u32[]{:S(2)}, u32[]{:S(2)}) %collective-permute-start.2) | collective-permute-done | bytes 2080 | tf_op jit(solution)/shard_map/while/body/eval_jaxpr/ppermute | solution.py:15
  224.0 1.9 bitcast_reduce_fusion.2
  225.9 1.1 fusion.38
  228.8 12.2 %collective-permute-done.2 = f32[64,1,8]{0,2,1:T(8,128)S(1)} collective-permute-done((f32[64,1,8]{0,2,1:T(8,128)S(1)}, f32[64,1,8]{0,2,1:T(8,128)S(1)}, u32[]{:S(2)}, u32[]{:S(2)}) %collective-permute-start.2) | collective-permute-done | bytes 2080 | tf_op jit(solution)/shard_map/while/body/eval_jaxpr/ppermute | solution.py:15
  241.8 1.9 bitcast_reduce_fusion.2
  243.7 1.1 fusion.38
  246.6 13.3 %collective-permute-done.2 = f32[64,1,8]{0,2,1:T(8,128)S(1)} collective-permute-done((f32[64,1,8]{0,2,1:T(8,128)S(1)}, f32[64,1,8]{0,2,1:T(8,128)S(1)}, u32[]{:S(2)}, u32[]{:S(2)}) %collective-permute-start.2) | collective-permute-done | bytes 2080 | tf_op jit(solution)/shard_map/while/body/eval_jaxpr/ppermute | solution.py:15
  260.6 1.9 bitcast_reduce_fusion.2
  262.6 1.1 fusion.38
  265.5 14.4 %collective-permute-done.2 = f32[64,1,8]{0,2,1:T(8,128)S(1)} collective-permute-done((f32[64,1,8]{0,2,1:T(8,128)S(1)}, f32[64,1,8]{0,2,1:T(8,128)S(1)}, u32[]{:S(2)}, u32[]{:S(2)}) %collective-permute-start.2) | collective-permute-done | bytes 2080 | tf_op jit(solution)/shard_map/while/body/eval_jaxpr/ppermute | solution.py:15
  280.0 1.3 fusion.21
  282.3 93.1 %all-gather.2.cloned.1.call-done = bf16[1024,1024]{1,0:T(8,128)(2,1)} async-done(((bf16[64,1024]{1,0:T(8,128)(2,1)}), bf16[1024,1024]{1,0:T(8,128)(2,1)}) %all-gather.2.cloned.1.call-update) | async-done | bytes 2097168 | tf_op jit(solution)/shard_map/all_gather | solution.py:76
  375.4 4.2 fusion.23
  379.6 35.2 %reduce-scatter.2.cloned.1.call-done = f32[128,512]{1,0:T(8,128)} async-done(((f32[1024,512]{1,0:T(8,128)}), f32[128,512]{1,0:T(8,128)}) %reduce-scatter.2.cloned.1.call-update) | async-done | bytes 262160 | tf_op jit(solution)/shard_map/reduce_scatter | solution.py:80
  (259 shorter events, 36.6 us)
Async XLA Ops:
  6.5 368.9 %all-gather.2.cloned.1.call-start = ((), (), s32[]{:S(2)}) async-start(), calls=%async_computation.1 | async-start | bytes 2228224 | tf_op jit(solution)/shard_map/all_gather | solution.py:76
  14.1 15.5 %collective-permute-start.1 = (f32[64,1,8,128]{3,2,0,1:T(8,128)S(1)}, f32[64,1,8,128]{3,2,0,1:T(8,128)S(1)}, u32[]{:S(2)}, u32[]{:S(2)}) collective-permute-start(f32[64,1,8,128]{3,2,0,1:T(8,128)S(1)} %fusion.40), channel_id=1, source_target_pairs={{0,16},{16,32},{32,48},{48,64},{64,80},{80,96},{96,112},{112,128},... | collective-permute-start | bytes 786440 | tf_op jit(solution)/shard_map/while/body/eval_jaxpr/ppermute | solution.py:15
  15.8 13.8 %collective-permute-start = (bf16[64,8,128]{2,0,1:T(8,128)(2,1)S(1)}, bf16[64,8,128]{2,0,1:T(8,128)(2,1)S(1)}, u32[]{:S(2)}, u32[]{:S(2)}) collective-permute-start(bf16[64,8,128]{2,0,1:T(8,128)(2,1)S(1)} %copy.30), channel_id=1, source_target_pairs={{0,16},{16,32},{32,48},{48,64},{64,80},{80,96},{96,112},{112,128},... | collective-permute-start | bytes 393224 | tf_op jit(solution)/shard_map/while/body/eval_jaxpr/ppermute | solution.py:15
  17.4 12.1 %collective-permute-start.2 = (f32[64,1,8]{0,2,1:T(8,128)S(1)}, f32[64,1,8]{0,2,1:T(8,128)S(1)}, u32[]{:S(2)}, u32[]{:S(2)}) collective-permute-start(f32[64,1,8]{0,2,1:T(8,128)S(1)} %get-tuple-element.155), channel_id=1, source_target_pairs={{0,16},{16,32},{32,48},{48,64},{64,80},{80,96},{96,112},{112,128},... | collective-permute-start | bytes 6152 | tf_op jit(solution)/shard_map/while/body/eval_jaxpr/ppermute | solution.py:15
  19.1 10.5 %collective-permute-start.3 = (f32[64,1,8]{0,2,1:T(8,128)S(1)}, f32[64,1,8]{0,2,1:T(8,128)S(1)}, u32[]{:S(2)}, u32[]{:S(2)}) collective-permute-start(f32[64,1,8]{0,2,1:T(8,128)S(1)} %get-tuple-element.156), channel_id=1, source_target_pairs={{0,16},{16,32},{32,48},{48,64},{64,80},{80,96},{96,112},{112,128},... | collective-permute-start | bytes 6152 | tf_op jit(solution)/shard_map/while/body/eval_jaxpr/ppermute | solution.py:15
  34.7 13.3 %collective-permute-start.1 = (f32[64,1,8,128]{3,2,0,1:T(8,128)S(1)}, f32[64,1,8,128]{3,2,0,1:T(8,128)S(1)}, u32[]{:S(2)}, u32[]{:S(2)}) collective-permute-start(f32[64,1,8,128]{3,2,0,1:T(8,128)S(1)} %fusion.40), channel_id=1, source_target_pairs={{0,16},{16,32},{32,48},{48,64},{64,80},{80,96},{96,112},{112,128},... | collective-permute-start | bytes 786440 | tf_op jit(solution)/shard_map/while/body/eval_jaxpr/ppermute | solution.py:15
  34.8 13.2 %collective-permute-start = (bf16[64,8,128]{2,0,1:T(8,128)(2,1)S(1)}, bf16[64,8,128]{2,0,1:T(8,128)(2,1)S(1)}, u32[]{:S(2)}, u32[]{:S(2)}) collective-permute-start(bf16[64,8,128]{2,0,1:T(8,128)(2,1)S(1)} %copy.30), channel_id=1, source_target_pairs={{0,16},{16,32},{32,48},{48,64},{64,80},{80,96},{96,112},{112,128},... | collective-permute-start | bytes 393224 | tf_op jit(solution)/shard_map/while/body/eval_jaxpr/ppermute | solution.py:15
  34.9 13.0 %collective-permute-start.2 = (f32[64,1,8]{0,2,1:T(8,128)S(1)}, f32[64,1,8]{0,2,1:T(8,128)S(1)}, u32[]{:S(2)}, u32[]{:S(2)}) collective-permute-start(f32[64,1,8]{0,2,1:T(8,128)S(1)} %get-tuple-element.155), channel_id=1, source_target_pairs={{0,16},{16,32},{32,48},{48,64},{64,80},{80,96},{96,112},{112,128},... | collective-permute-start | bytes 6152 | tf_op jit(solution)/shard_map/while/body/eval_jaxpr/ppermute | solution.py:15
  35.1 12.9 %collective-permute-start.3 = (f32[64,1,8]{0,2,1:T(8,128)S(1)}, f32[64,1,8]{0,2,1:T(8,128)S(1)}, u32[]{:S(2)}, u32[]{:S(2)}) collective-permute-start(f32[64,1,8]{0,2,1:T(8,128)S(1)} %get-tuple-element.156), channel_id=1, source_target_pairs={{0,16},{16,32},{32,48},{48,64},{64,80},{80,96},{96,112},{112,128},... | collective-permute-start | bytes 6152 | tf_op jit(solution)/shard_map/while/body/eval_jaxpr/ppermute | solution.py:15
  53.1 12.3 %collective-permute-start.1 = (f32[64,1,8,128]{3,2,0,1:T(8,128)S(1)}, f32[64,1,8,128]{3,2,0,1:T(8,128)S(1)}, u32[]{:S(2)}, u32[]{:S(2)}) collective-permute-start(f32[64,1,8,128]{3,2,0,1:T(8,128)S(1)} %fusion.40), channel_id=1, source_target_pairs={{0,16},{16,32},{32,48},{48,64},{64,80},{80,96},{96,112},{112,128},... | collective-permute-start | bytes 786440 | tf_op jit(solution)/shard_map/while/body/eval_jaxpr/ppermute | solution.py:15
  53.2 12.2 %collective-permute-start = (bf16[64,8,128]{2,0,1:T(8,128)(2,1)S(1)}, bf16[64,8,128]{2,0,1:T(8,128)(2,1)S(1)}, u32[]{:S(2)}, u32[]{:S(2)}) collective-permute-start(bf16[64,8,128]{2,0,1:T(8,128)(2,1)S(1)} %copy.30), channel_id=1, source_target_pairs={{0,16},{16,32},{32,48},{48,64},{64,80},{80,96},{96,112},{112,128},... | collective-permute-start | bytes 393224 | tf_op jit(solution)/shard_map/while/body/eval_jaxpr/ppermute | solution.py:15
  53.3 12.0 %collective-permute-start.2 = (f32[64,1,8]{0,2,1:T(8,128)S(1)}, f32[64,1,8]{0,2,1:T(8,128)S(1)}, u32[]{:S(2)}, u32[]{:S(2)}) collective-permute-start(f32[64,1,8]{0,2,1:T(8,128)S(1)} %get-tuple-element.155), channel_id=1, source_target_pairs={{0,16},{16,32},{32,48},{48,64},{64,80},{80,96},{96,112},{112,128},... | collective-permute-start | bytes 6152 | tf_op jit(solution)/shard_map/while/body/eval_jaxpr/ppermute | solution.py:15
  53.4 12.0 %collective-permute-start.3 = (f32[64,1,8]{0,2,1:T(8,128)S(1)}, f32[64,1,8]{0,2,1:T(8,128)S(1)}, u32[]{:S(2)}, u32[]{:S(2)}) collective-permute-start(f32[64,1,8]{0,2,1:T(8,128)S(1)} %get-tuple-element.156), channel_id=1, source_target_pairs={{0,16},{16,32},{32,48},{48,64},{64,80},{80,96},{96,112},{112,128},... | collective-permute-start | bytes 6152 | tf_op jit(solution)/shard_map/while/body/eval_jaxpr/ppermute | solution.py:15
  70.6 11.4 %collective-permute-start.1 = (f32[64,1,8,128]{3,2,0,1:T(8,128)S(1)}, f32[64,1,8,128]{3,2,0,1:T(8,128)S(1)}, u32[]{:S(2)}, u32[]{:S(2)}) collective-permute-start(f32[64,1,8,128]{3,2,0,1:T(8,128)S(1)} %fusion.40), channel_id=1, source_target_pairs={{0,16},{16,32},{32,48},{48,64},{64,80},{80,96},{96,112},{112,128},... | collective-permute-start | bytes 786440 | tf_op jit(solution)/shard_map/while/body/eval_jaxpr/ppermute | solution.py:15
  70.7 11.3 %collective-permute-start = (bf16[64,8,128]{2,0,1:T(8,128)(2,1)S(1)}, bf16[64,8,128]{2,0,1:T(8,128)(2,1)S(1)}, u32[]{:S(2)}, u32[]{:S(2)}) collective-permute-start(bf16[64,8,128]{2,0,1:T(8,128)(2,1)S(1)} %copy.30), channel_id=1, source_target_pairs={{0,16},{16,32},{32,48},{48,64},{64,80},{80,96},{96,112},{112,128},... | collective-permute-start | bytes 393224 | tf_op jit(solution)/shard_map/while/body/eval_jaxpr/ppermute | solution.py:15
  70.8 11.1 %collective-permute-start.2 = (f32[64,1,8]{0,2,1:T(8,128)S(1)}, f32[64,1,8]{0,2,1:T(8,128)S(1)}, u32[]{:S(2)}, u32[]{:S(2)}) collective-permute-start(f32[64,1,8]{0,2,1:T(8,128)S(1)} %get-tuple-element.155), channel_id=1, source_target_pairs={{0,16},{16,32},{32,48},{48,64},{64,80},{80,96},{96,112},{112,128},... | collective-permute-start | bytes 6152 | tf_op jit(solution)/shard_map/while/body/eval_jaxpr/ppermute | solution.py:15
  70.9 11.1 %collective-permute-start.3 = (f32[64,1,8]{0,2,1:T(8,128)S(1)}, f32[64,1,8]{0,2,1:T(8,128)S(1)}, u32[]{:S(2)}, u32[]{:S(2)}) collective-permute-start(f32[64,1,8]{0,2,1:T(8,128)S(1)} %get-tuple-element.156), channel_id=1, source_target_pairs={{0,16},{16,32},{32,48},{48,64},{64,80},{80,96},{96,112},{112,128},... | collective-permute-start | bytes 6152 | tf_op jit(solution)/shard_map/while/body/eval_jaxpr/ppermute | solution.py:15
  87.2 10.4 %collective-permute-start.1 = (f32[64,1,8,128]{3,2,0,1:T(8,128)S(1)}, f32[64,1,8,128]{3,2,0,1:T(8,128)S(1)}, u32[]{:S(2)}, u32[]{:S(2)}) collective-permute-start(f32[64,1,8,128]{3,2,0,1:T(8,128)S(1)} %fusion.40), channel_id=1, source_target_pairs={{0,16},{16,32},{32,48},{48,64},{64,80},{80,96},{96,112},{112,128},... | collective-permute-start | bytes 786440 | tf_op jit(solution)/shard_map/while/body/eval_jaxpr/ppermute | solution.py:15
  87.2 10.3 %collective-permute-start = (bf16[64,8,128]{2,0,1:T(8,128)(2,1)S(1)}, bf16[64,8,128]{2,0,1:T(8,128)(2,1)S(1)}, u32[]{:S(2)}, u32[]{:S(2)}) collective-permute-start(bf16[64,8,128]{2,0,1:T(8,128)(2,1)S(1)} %copy.30), channel_id=1, source_target_pairs={{0,16},{16,32},{32,48},{48,64},{64,80},{80,96},{96,112},{112,128},... | collective-permute-start | bytes 393224 | tf_op jit(solution)/shard_map/while/body/eval_jaxpr/ppermute | solution.py:15
  87.3 10.2 %collective-permute-start.2 = (f32[64,1,8]{0,2,1:T(8,128)S(1)}, f32[64,1,8]{0,2,1:T(8,128)S(1)}, u32[]{:S(2)}, u32[]{:S(2)}) collective-permute-start(f32[64,1,8]{0,2,1:T(8,128)S(1)} %get-tuple-element.155), channel_id=1, source_target_pairs={{0,16},{16,32},{32,48},{48,64},{64,80},{80,96},{96,112},{112,128},... | collective-permute-start | bytes 6152 | tf_op jit(solution)/shard_map/while/body/eval_jaxpr/ppermute | solution.py:15
  87.4 10.1 %collective-permute-start.3 = (f32[64,1,8]{0,2,1:T(8,128)S(1)}, f32[64,1,8]{0,2,1:T(8,128)S(1)}, u32[]{:S(2)}, u32[]{:S(2)}) collective-permute-start(f32[64,1,8]{0,2,1:T(8,128)S(1)} %get-tuple-element.156), channel_id=1, source_target_pairs={{0,16},{16,32},{32,48},{48,64},{64,80},{80,96},{96,112},{112,128},... | collective-permute-start | bytes 6152 | tf_op jit(solution)/shard_map/while/body/eval_jaxpr/ppermute | solution.py:15
  102.7 10.4 %collective-permute-start.1 = (f32[64,1,8,128]{3,2,0,1:T(8,128)S(1)}, f32[64,1,8,128]{3,2,0,1:T(8,128)S(1)}, u32[]{:S(2)}, u32[]{:S(2)}) collective-permute-start(f32[64,1,8,128]{3,2,0,1:T(8,128)S(1)} %fusion.40), channel_id=1, source_target_pairs={{0,16},{16,32},{32,48},{48,64},{64,80},{80,96},{96,112},{112,128},... | collective-permute-start | bytes 786440 | tf_op jit(solution)/shard_map/while/body/eval_jaxpr/ppermute | solution.py:15
  102.8 10.3 %collective-permute-start = (bf16[64,8,128]{2,0,1:T(8,128)(2,1)S(1)}, bf16[64,8,128]{2,0,1:T(8,128)(2,1)S(1)}, u32[]{:S(2)}, u32[]{:S(2)}) collective-permute-start(bf16[64,8,128]{2,0,1:T(8,128)(2,1)S(1)} %copy.30), channel_id=1, source_target_pairs={{0,16},{16,32},{32,48},{48,64},{64,80},{80,96},{96,112},{112,128},... | collective-permute-start | bytes 393224 | tf_op jit(solution)/shard_map/while/body/eval_jaxpr/ppermute | solution.py:15
  102.9 10.2 %collective-permute-start.2 = (f32[64,1,8]{0,2,1:T(8,128)S(1)}, f32[64,1,8]{0,2,1:T(8,128)S(1)}, u32[]{:S(2)}, u32[]{:S(2)}) collective-permute-start(f32[64,1,8]{0,2,1:T(8,128)S(1)} %get-tuple-element.155), channel_id=1, source_target_pairs={{0,16},{16,32},{32,48},{48,64},{64,80},{80,96},{96,112},{112,128},... | collective-permute-start | bytes 6152 | tf_op jit(solution)/shard_map/while/body/eval_jaxpr/ppermute | solution.py:15
  103.0 10.1 %collective-permute-start.3 = (f32[64,1,8]{0,2,1:T(8,128)S(1)}, f32[64,1,8]{0,2,1:T(8,128)S(1)}, u32[]{:S(2)}, u32[]{:S(2)}) collective-permute-start(f32[64,1,8]{0,2,1:T(8,128)S(1)} %get-tuple-element.156), channel_id=1, source_target_pairs={{0,16},{16,32},{32,48},{48,64},{64,80},{80,96},{96,112},{112,128},... | collective-permute-start | bytes 6152 | tf_op jit(solution)/shard_map/while/body/eval_jaxpr/ppermute | solution.py:15
  118.3 10.4 %collective-permute-start.1 = (f32[64,1,8,128]{3,2,0,1:T(8,128)S(1)}, f32[64,1,8,128]{3,2,0,1:T(8,128)S(1)}, u32[]{:S(2)}, u32[]{:S(2)}) collective-permute-start(f32[64,1,8,128]{3,2,0,1:T(8,128)S(1)} %fusion.40), channel_id=1, source_target_pairs={{0,16},{16,32},{32,48},{48,64},{64,80},{80,96},{96,112},{112,128},... | collective-permute-start | bytes 786440 | tf_op jit(solution)/shard_map/while/body/eval_jaxpr/ppermute | solution.py:15
  118.4 10.3 %collective-permute-start = (bf16[64,8,128]{2,0,1:T(8,128)(2,1)S(1)}, bf16[64,8,128]{2,0,1:T(8,128)(2,1)S(1)}, u32[]{:S(2)}, u32[]{:S(2)}) collective-permute-start(bf16[64,8,128]{2,0,1:T(8,128)(2,1)S(1)} %copy.30), channel_id=1, source_target_pairs={{0,16},{16,32},{32,48},{48,64},{64,80},{80,96},{96,112},{112,128},... | collective-permute-start | bytes 393224 | tf_op jit(solution)/shard_map/while/body/eval_jaxpr/ppermute | solution.py:15
  118.5 10.2 %collective-permute-start.2 = (f32[64,1,8]{0,2,1:T(8,128)S(1)}, f32[64,1,8]{0,2,1:T(8,128)S(1)}, u32[]{:S(2)}, u32[]{:S(2)}) collective-permute-start(f32[64,1,8]{0,2,1:T(8,128)S(1)} %get-tuple-element.155), channel_id=1, source_target_pairs={{0,16},{16,32},{32,48},{48,64},{64,80},{80,96},{96,112},{112,128},... | collective-permute-start | bytes 6152 | tf_op jit(solution)/shard_map/while/body/eval_jaxpr/ppermute | solution.py:15
  118.6 10.1 %collective-permute-start.3 = (f32[64,1,8]{0,2,1:T(8,128)S(1)}, f32[64,1,8]{0,2,1:T(8,128)S(1)}, u32[]{:S(2)}, u32[]{:S(2)}) collective-permute-start(f32[64,1,8]{0,2,1:T(8,128)S(1)} %get-tuple-element.156), channel_id=1, source_target_pairs={{0,16},{16,32},{32,48},{48,64},{64,80},{80,96},{96,112},{112,128},... | collective-permute-start | bytes 6152 | tf_op jit(solution)/shard_map/while/body/eval_jaxpr/ppermute | solution.py:15
  133.8 10.4 %collective-permute-start.1 = (f32[64,1,8,128]{3,2,0,1:T(8,128)S(1)}, f32[64,1,8,128]{3,2,0,1:T(8,128)S(1)}, u32[]{:S(2)}, u32[]{:S(2)}) collective-permute-start(f32[64,1,8,128]{3,2,0,1:T(8,128)S(1)} %fusion.40), channel_id=1, source_target_pairs={{0,16},{16,32},{32,48},{48,64},{64,80},{80,96},{96,112},{112,128},... | collective-permute-start | bytes 786440 | tf_op jit(solution)/shard_map/while/body/eval_jaxpr/ppermute | solution.py:15
  133.9 10.3 %collective-permute-start = (bf16[64,8,128]{2,0,1:T(8,128)(2,1)S(1)}, bf16[64,8,128]{2,0,1:T(8,128)(2,1)S(1)}, u32[]{:S(2)}, u32[]{:S(2)}) collective-permute-start(bf16[64,8,128]{2,0,1:T(8,128)(2,1)S(1)} %copy.30), channel_id=1, source_target_pairs={{0,16},{16,32},{32,48},{48,64},{64,80},{80,96},{96,112},{112,128},... | collective-permute-start | bytes 393224 | tf_op jit(solution)/shard_map/while/body/eval_jaxpr/ppermute | solution.py:15
  134.0 10.2 %collective-permute-start.2 = (f32[64,1,8]{0,2,1:T(8,128)S(1)}, f32[64,1,8]{0,2,1:T(8,128)S(1)}, u32[]{:S(2)}, u32[]{:S(2)}) collective-permute-start(f32[64,1,8]{0,2,1:T(8,128)S(1)} %get-tuple-element.155), channel_id=1, source_target_pairs={{0,16},{16,32},{32,48},{48,64},{64,80},{80,96},{96,112},{112,128},... | collective-permute-start | bytes 6152 | tf_op jit(solution)/shard_map/while/body/eval_jaxpr/ppermute | solution.py:15
  134.1 10.1 %collective-permute-start.3 = (f32[64,1,8]{0,2,1:T(8,128)S(1)}, f32[64,1,8]{0,2,1:T(8,128)S(1)}, u32[]{:S(2)}, u32[]{:S(2)}) collective-permute-start(f32[64,1,8]{0,2,1:T(8,128)S(1)} %get-tuple-element.156), channel_id=1, source_target_pairs={{0,16},{16,32},{32,48},{48,64},{64,80},{80,96},{96,112},{112,128},... | collective-permute-start | bytes 6152 | tf_op jit(solution)/shard_map/while/body/eval_jaxpr/ppermute | solution.py:15
  149.4 10.4 %collective-permute-start.1 = (f32[64,1,8,128]{3,2,0,1:T(8,128)S(1)}, f32[64,1,8,128]{3,2,0,1:T(8,128)S(1)}, u32[]{:S(2)}, u32[]{:S(2)}) collective-permute-start(f32[64,1,8,128]{3,2,0,1:T(8,128)S(1)} %fusion.40), channel_id=1, source_target_pairs={{0,16},{16,32},{32,48},{48,64},{64,80},{80,96},{96,112},{112,128},... | collective-permute-start | bytes 786440 | tf_op jit(solution)/shard_map/while/body/eval_jaxpr/ppermute | solution.py:15
  149.5 10.3 %collective-permute-start = (bf16[64,8,128]{2,0,1:T(8,128)(2,1)S(1)}, bf16[64,8,128]{2,0,1:T(8,128)(2,1)S(1)}, u32[]{:S(2)}, u32[]{:S(2)}) collective-permute-start(bf16[64,8,128]{2,0,1:T(8,128)(2,1)S(1)} %copy.30), channel_id=1, source_target_pairs={{0,16},{16,32},{32,48},{48,64},{64,80},{80,96},{96,112},{112,128},... | collective-permute-start | bytes 393224 | tf_op jit(solution)/shard_map/while/body/eval_jaxpr/ppermute | solution.py:15
  149.6 10.2 %collective-permute-start.2 = (f32[64,1,8]{0,2,1:T(8,128)S(1)}, f32[64,1,8]{0,2,1:T(8,128)S(1)}, u32[]{:S(2)}, u32[]{:S(2)}) collective-permute-start(f32[64,1,8]{0,2,1:T(8,128)S(1)} %get-tuple-element.155), channel_id=1, source_target_pairs={{0,16},{16,32},{32,48},{48,64},{64,80},{80,96},{96,112},{112,128},... | collective-permute-start | bytes 6152 | tf_op jit(solution)/shard_map/while/body/eval_jaxpr/ppermute | solution.py:15
  149.7 10.1 %collective-permute-start.3 = (f32[64,1,8]{0,2,1:T(8,128)S(1)}, f32[64,1,8]{0,2,1:T(8,128)S(1)}, u32[]{:S(2)}, u32[]{:S(2)}) collective-permute-start(f32[64,1,8]{0,2,1:T(8,128)S(1)} %get-tuple-element.156), channel_id=1, source_target_pairs={{0,16},{16,32},{32,48},{48,64},{64,80},{80,96},{96,112},{112,128},... | collective-permute-start | bytes 6152 | tf_op jit(solution)/shard_map/while/body/eval_jaxpr/ppermute | solution.py:15
  165.0 10.4 %collective-permute-start.1 = (f32[64,1,8,128]{3,2,0,1:T(8,128)S(1)}, f32[64,1,8,128]{3,2,0,1:T(8,128)S(1)}, u32[]{:S(2)}, u32[]{:S(2)}) collective-permute-start(f32[64,1,8,128]{3,2,0,1:T(8,128)S(1)} %fusion.40), channel_id=1, source_target_pairs={{0,16},{16,32},{32,48},{48,64},{64,80},{80,96},{96,112},{112,128},... | collective-permute-start | bytes 786440 | tf_op jit(solution)/shard_map/while/body/eval_jaxpr/ppermute | solution.py:15
  165.1 10.3 %collective-permute-start = (bf16[64,8,128]{2,0,1:T(8,128)(2,1)S(1)}, bf16[64,8,128]{2,0,1:T(8,128)(2,1)S(1)}, u32[]{:S(2)}, u32[]{:S(2)}) collective-permute-start(bf16[64,8,128]{2,0,1:T(8,128)(2,1)S(1)} %copy.30), channel_id=1, source_target_pairs={{0,16},{16,32},{32,48},{48,64},{64,80},{80,96},{96,112},{112,128},... | collective-permute-start | bytes 393224 | tf_op jit(solution)/shard_map/while/body/eval_jaxpr/ppermute | solution.py:15
  165.1 10.2 %collective-permute-start.2 = (f32[64,1,8]{0,2,1:T(8,128)S(1)}, f32[64,1,8]{0,2,1:T(8,128)S(1)}, u32[]{:S(2)}, u32[]{:S(2)}) collective-permute-start(f32[64,1,8]{0,2,1:T(8,128)S(1)} %get-tuple-element.155), channel_id=1, source_target_pairs={{0,16},{16,32},{32,48},{48,64},{64,80},{80,96},{96,112},{112,128},... | collective-permute-start | bytes 6152 | tf_op jit(solution)/shard_map/while/body/eval_jaxpr/ppermute | solution.py:15
  180.5 10.4 %collective-permute-start.1 = (f32[64,1,8,128]{3,2,0,1:T(8,128)S(1)}, f32[64,1,8,128]{3,2,0,1:T(8,128)S(1)}, u32[]{:S(2)}, u32[]{:S(2)}) collective-permute-start(f32[64,1,8,128]{3,2,0,1:T(8,128)S(1)} %fusion.40), channel_id=1, source_target_pairs={{0,16},{16,32},{32,48},{48,64},{64,80},{80,96},{96,112},{112,128},... | collective-permute-start | bytes 786440 | tf_op jit(solution)/shard_map/while/body/eval_jaxpr/ppermute | solution.py:15
  180.6 10.3 %collective-permute-start = (bf16[64,8,128]{2,0,1:T(8,128)(2,1)S(1)}, bf16[64,8,128]{2,0,1:T(8,128)(2,1)S(1)}, u32[]{:S(2)}, u32[]{:S(2)}) collective-permute-start(bf16[64,8,128]{2,0,1:T(8,128)(2,1)S(1)} %copy.30), channel_id=1, source_target_pairs={{0,16},{16,32},{32,48},{48,64},{64,80},{80,96},{96,112},{112,128},... | collective-permute-start | bytes 393224 | tf_op jit(solution)/shard_map/while/body/eval_jaxpr/ppermute | solution.py:15
  180.7 10.2 %collective-permute-start.2 = (f32[64,1,8]{0,2,1:T(8,128)S(1)}, f32[64,1,8]{0,2,1:T(8,128)S(1)}, u32[]{:S(2)}, u32[]{:S(2)}) collective-permute-start(f32[64,1,8]{0,2,1:T(8,128)S(1)} %get-tuple-element.155), channel_id=1, source_target_pairs={{0,16},{16,32},{32,48},{48,64},{64,80},{80,96},{96,112},{112,128},... | collective-permute-start | bytes 6152 | tf_op jit(solution)/shard_map/while/body/eval_jaxpr/ppermute | solution.py:15
  196.1 10.5 %collective-permute-start.1 = (f32[64,1,8,128]{3,2,0,1:T(8,128)S(1)}, f32[64,1,8,128]{3,2,0,1:T(8,128)S(1)}, u32[]{:S(2)}, u32[]{:S(2)}) collective-permute-start(f32[64,1,8,128]{3,2,0,1:T(8,128)S(1)} %fusion.40), channel_id=1, source_target_pairs={{0,16},{16,32},{32,48},{48,64},{64,80},{80,96},{96,112},{112,128},... | collective-permute-start | bytes 786440 | tf_op jit(solution)/shard_map/while/body/eval_jaxpr/ppermute | solution.py:15
  196.2 10.4 %collective-permute-start = (bf16[64,8,128]{2,0,1:T(8,128)(2,1)S(1)}, bf16[64,8,128]{2,0,1:T(8,128)(2,1)S(1)}, u32[]{:S(2)}, u32[]{:S(2)}) collective-permute-start(bf16[64,8,128]{2,0,1:T(8,128)(2,1)S(1)} %copy.30), channel_id=1, source_target_pairs={{0,16},{16,32},{32,48},{48,64},{64,80},{80,96},{96,112},{112,128},... | collective-permute-start | bytes 393224 | tf_op jit(solution)/shard_map/while/body/eval_jaxpr/ppermute | solution.py:15
  196.3 10.3 %collective-permute-start.2 = (f32[64,1,8]{0,2,1:T(8,128)S(1)}, f32[64,1,8]{0,2,1:T(8,128)S(1)}, u32[]{:S(2)}, u32[]{:S(2)}) collective-permute-start(f32[64,1,8]{0,2,1:T(8,128)S(1)} %get-tuple-element.155), channel_id=1, source_target_pairs={{0,16},{16,32},{32,48},{48,64},{64,80},{80,96},{96,112},{112,128},... | collective-permute-start | bytes 6152 | tf_op jit(solution)/shard_map/while/body/eval_jaxpr/ppermute | solution.py:15
  196.4 10.2 %collective-permute-start.3 = (f32[64,1,8]{0,2,1:T(8,128)S(1)}, f32[64,1,8]{0,2,1:T(8,128)S(1)}, u32[]{:S(2)}, u32[]{:S(2)}) collective-permute-start(f32[64,1,8]{0,2,1:T(8,128)S(1)} %get-tuple-element.156), channel_id=1, source_target_pairs={{0,16},{16,32},{32,48},{48,64},{64,80},{80,96},{96,112},{112,128},... | collective-permute-start | bytes 6152 | tf_op jit(solution)/shard_map/while/body/eval_jaxpr/ppermute | solution.py:15
  211.7 11.6 %collective-permute-start.1 = (f32[64,1,8,128]{3,2,0,1:T(8,128)S(1)}, f32[64,1,8,128]{3,2,0,1:T(8,128)S(1)}, u32[]{:S(2)}, u32[]{:S(2)}) collective-permute-start(f32[64,1,8,128]{3,2,0,1:T(8,128)S(1)} %fusion.40), channel_id=1, source_target_pairs={{0,16},{16,32},{32,48},{48,64},{64,80},{80,96},{96,112},{112,128},... | collective-permute-start | bytes 786440 | tf_op jit(solution)/shard_map/while/body/eval_jaxpr/ppermute | solution.py:15
  211.8 11.5 %collective-permute-start = (bf16[64,8,128]{2,0,1:T(8,128)(2,1)S(1)}, bf16[64,8,128]{2,0,1:T(8,128)(2,1)S(1)}, u32[]{:S(2)}, u32[]{:S(2)}) collective-permute-start(bf16[64,8,128]{2,0,1:T(8,128)(2,1)S(1)} %copy.30), channel_id=1, source_target_pairs={{0,16},{16,32},{32,48},{48,64},{64,80},{80,96},{96,112},{112,128},... | collective-permute-start | bytes 393224 | tf_op jit(solution)/shard_map/while/body/eval_jaxpr/ppermute | solution.py:15
  211.9 11.3 %collective-permute-start.2 = (f32[64,1,8]{0,2,1:T(8,128)S(1)}, f32[64,1,8]{0,2,1:T(8,128)S(1)}, u32[]{:S(2)}, u32[]{:S(2)}) collective-permute-start(f32[64,1,8]{0,2,1:T(8,128)S(1)} %get-tuple-element.155), channel_id=1, source_target_pairs={{0,16},{16,32},{32,48},{48,64},{64,80},{80,96},{96,112},{112,128},... | collective-permute-start | bytes 6152 | tf_op jit(solution)/shard_map/while/body/eval_jaxpr/ppermute | solution.py:15
  212.0 11.3 %collective-permute-start.3 = (f32[64,1,8]{0,2,1:T(8,128)S(1)}, f32[64,1,8]{0,2,1:T(8,128)S(1)}, u32[]{:S(2)}, u32[]{:S(2)}) collective-permute-start(f32[64,1,8]{0,2,1:T(8,128)S(1)} %get-tuple-element.156), channel_id=1, source_target_pairs={{0,16},{16,32},{32,48},{48,64},{64,80},{80,96},{96,112},{112,128},... | collective-permute-start | bytes 6152 | tf_op jit(solution)/shard_map/while/body/eval_jaxpr/ppermute | solution.py:15
  228.4 12.6 %collective-permute-start.1 = (f32[64,1,8,128]{3,2,0,1:T(8,128)S(1)}, f32[64,1,8,128]{3,2,0,1:T(8,128)S(1)}, u32[]{:S(2)}, u32[]{:S(2)}) collective-permute-start(f32[64,1,8,128]{3,2,0,1:T(8,128)S(1)} %fusion.40), channel_id=1, source_target_pairs={{0,16},{16,32},{32,48},{48,64},{64,80},{80,96},{96,112},{112,128},... | collective-permute-start | bytes 786440 | tf_op jit(solution)/shard_map/while/body/eval_jaxpr/ppermute | solution.py:15
  228.5 12.6 %collective-permute-start = (bf16[64,8,128]{2,0,1:T(8,128)(2,1)S(1)}, bf16[64,8,128]{2,0,1:T(8,128)(2,1)S(1)}, u32[]{:S(2)}, u32[]{:S(2)}) collective-permute-start(bf16[64,8,128]{2,0,1:T(8,128)(2,1)S(1)} %copy.30), channel_id=1, source_target_pairs={{0,16},{16,32},{32,48},{48,64},{64,80},{80,96},{96,112},{112,128},... | collective-permute-start | bytes 393224 | tf_op jit(solution)/shard_map/while/body/eval_jaxpr/ppermute | solution.py:15
  228.6 12.4 %collective-permute-start.2 = (f32[64,1,8]{0,2,1:T(8,128)S(1)}, f32[64,1,8]{0,2,1:T(8,128)S(1)}, u32[]{:S(2)}, u32[]{:S(2)}) collective-permute-start(f32[64,1,8]{0,2,1:T(8,128)S(1)} %get-tuple-element.155), channel_id=1, source_target_pairs={{0,16},{16,32},{32,48},{48,64},{64,80},{80,96},{96,112},{112,128},... | collective-permute-start | bytes 6152 | tf_op jit(solution)/shard_map/while/body/eval_jaxpr/ppermute | solution.py:15
  228.7 12.4 %collective-permute-start.3 = (f32[64,1,8]{0,2,1:T(8,128)S(1)}, f32[64,1,8]{0,2,1:T(8,128)S(1)}, u32[]{:S(2)}, u32[]{:S(2)}) collective-permute-start(f32[64,1,8]{0,2,1:T(8,128)S(1)} %get-tuple-element.156), channel_id=1, source_target_pairs={{0,16},{16,32},{32,48},{48,64},{64,80},{80,96},{96,112},{112,128},... | collective-permute-start | bytes 6152 | tf_op jit(solution)/shard_map/while/body/eval_jaxpr/ppermute | solution.py:15
  246.2 13.7 %collective-permute-start.1 = (f32[64,1,8,128]{3,2,0,1:T(8,128)S(1)}, f32[64,1,8,128]{3,2,0,1:T(8,128)S(1)}, u32[]{:S(2)}, u32[]{:S(2)}) collective-permute-start(f32[64,1,8,128]{3,2,0,1:T(8,128)S(1)} %fusion.40), channel_id=1, source_target_pairs={{0,16},{16,32},{32,48},{48,64},{64,80},{80,96},{96,112},{112,128},... | collective-permute-start | bytes 786440 | tf_op jit(solution)/shard_map/while/body/eval_jaxpr/ppermute | solution.py:15
  246.3 13.6 %collective-permute-start = (bf16[64,8,128]{2,0,1:T(8,128)(2,1)S(1)}, bf16[64,8,128]{2,0,1:T(8,128)(2,1)S(1)}, u32[]{:S(2)}, u32[]{:S(2)}) collective-permute-start(bf16[64,8,128]{2,0,1:T(8,128)(2,1)S(1)} %copy.30), channel_id=1, source_target_pairs={{0,16},{16,32},{32,48},{48,64},{64,80},{80,96},{96,112},{112,128},... | collective-permute-start | bytes 393224 | tf_op jit(solution)/shard_map/while/body/eval_jaxpr/ppermute | solution.py:15
  246.4 13.5 %collective-permute-start.2 = (f32[64,1,8]{0,2,1:T(8,128)S(1)}, f32[64,1,8]{0,2,1:T(8,128)S(1)}, u32[]{:S(2)}, u32[]{:S(2)}) collective-permute-start(f32[64,1,8]{0,2,1:T(8,128)S(1)} %get-tuple-element.155), channel_id=1, source_target_pairs={{0,16},{16,32},{32,48},{48,64},{64,80},{80,96},{96,112},{112,128},... | collective-permute-start | bytes 6152 | tf_op jit(solution)/shard_map/while/body/eval_jaxpr/ppermute | solution.py:15
  246.5 13.5 %collective-permute-start.3 = (f32[64,1,8]{0,2,1:T(8,128)S(1)}, f32[64,1,8]{0,2,1:T(8,128)S(1)}, u32[]{:S(2)}, u32[]{:S(2)}) collective-permute-start(f32[64,1,8]{0,2,1:T(8,128)S(1)} %get-tuple-element.156), channel_id=1, source_target_pairs={{0,16},{16,32},{32,48},{48,64},{64,80},{80,96},{96,112},{112,128},... | collective-permute-start | bytes 6152 | tf_op jit(solution)/shard_map/while/body/eval_jaxpr/ppermute | solution.py:15
  265.1 14.8 %collective-permute-start.1 = (f32[64,1,8,128]{3,2,0,1:T(8,128)S(1)}, f32[64,1,8,128]{3,2,0,1:T(8,128)S(1)}, u32[]{:S(2)}, u32[]{:S(2)}) collective-permute-start(f32[64,1,8,128]{3,2,0,1:T(8,128)S(1)} %fusion.40), channel_id=1, source_target_pairs={{0,16},{16,32},{32,48},{48,64},{64,80},{80,96},{96,112},{112,128},... | collective-permute-start | bytes 786440 | tf_op jit(solution)/shard_map/while/body/eval_jaxpr/ppermute | solution.py:15
  265.2 14.7 %collective-permute-start = (bf16[64,8,128]{2,0,1:T(8,128)(2,1)S(1)}, bf16[64,8,128]{2,0,1:T(8,128)(2,1)S(1)}, u32[]{:S(2)}, u32[]{:S(2)}) collective-permute-start(bf16[64,8,128]{2,0,1:T(8,128)(2,1)S(1)} %copy.30), channel_id=1, source_target_pairs={{0,16},{16,32},{32,48},{48,64},{64,80},{80,96},{96,112},{112,128},... | collective-permute-start | bytes 393224 | tf_op jit(solution)/shard_map/while/body/eval_jaxpr/ppermute | solution.py:15
  265.3 14.6 %collective-permute-start.2 = (f32[64,1,8]{0,2,1:T(8,128)S(1)}, f32[64,1,8]{0,2,1:T(8,128)S(1)}, u32[]{:S(2)}, u32[]{:S(2)}) collective-permute-start(f32[64,1,8]{0,2,1:T(8,128)S(1)} %get-tuple-element.155), channel_id=1, source_target_pairs={{0,16},{16,32},{32,48},{48,64},{64,80},{80,96},{96,112},{112,128},... | collective-permute-start | bytes 6152 | tf_op jit(solution)/shard_map/while/body/eval_jaxpr/ppermute | solution.py:15
  265.4 14.6 %collective-permute-start.3 = (f32[64,1,8]{0,2,1:T(8,128)S(1)}, f32[64,1,8]{0,2,1:T(8,128)S(1)}, u32[]{:S(2)}, u32[]{:S(2)}) collective-permute-start(f32[64,1,8]{0,2,1:T(8,128)S(1)} %get-tuple-element.156), channel_id=1, source_target_pairs={{0,16},{16,32},{32,48},{48,64},{64,80},{80,96},{96,112},{112,128},... | collective-permute-start | bytes 6152 | tf_op jit(solution)/shard_map/while/body/eval_jaxpr/ppermute | solution.py:15
  282.3 132.5 %reduce-scatter.2.cloned.1.call-start = ((), (), s32[]{:S(2)}) async-start(), calls=%async_computation.2 | async-start | bytes 2359296 | tf_op jit(solution)/shard_map/reduce_scatter | solution.py:80
  (19 other events, 438.3 us)
Sparse Core Ops, SparseCore 0:
  282.4 92.9 all-gather.1
  379.7 35.0 reduce-scatter.1
where the time goes:
time: 425 us; the launch traced here: 422 us
  waiting for transfers between devices  300 us (71%)
  matrix products  51 us (12%)
  other arithmetic  33.3 us (8%)
  starting transfers between devices  17 us (4%)
  between operations  13.4 us (3%)
  local copies, waits for them, and re-layouts  6.05 us (1%)
    ppermute x64, waiting for transfers between devices, shifted(): return lax.ppermute(value, axis, pairs)  171 us
    all_gather x1, waiting for transfers between devices, body(): lax.all_gather(mixed, 'ctx', axis=0, tiled=True)  93.1 us
    reduce_scatter x1, waiting for transfers between devices, body(): lax.psum_scatter(partial_sums, 'head', scatter_dimension=0, tiled=True)  35.2 us
    dot_general x16, matrix products, block_terms(): jnp.einsum('qgjd,kgd->qgjk', grouped, keys, preferred_element_type=jnp.fl...  31.1 us
    reduce_sum x16, other arithmetic, block_terms(): total = jnp.sum(weights, axis=3)  17.7 us
    ppermute x64, starting transfers between devices, shifted(): return lax.ppermute(value, axis, pairs)  17 us
    dot_general x16, matrix products, block_terms(): jnp.einsum('qgjk,kgd->qgjd', weights.astype(jnp.bfloat16), values, prefer...  15.7 us
    lt x16, other arithmetic, block_terms(): visible = (key_pos < prompt_lengths[0])[None, None, None, :]  10.5 us
  transfers between devices with their start and end apart: 66, of which 23 were waited for; matrix products, arithmetic and copies ran while one was open for 0% of the time, Pallas kernels for 0%

commit v1 on v0

v1 whole, which is shorter than its diff:
```python
import functools

import jax
import jax.numpy as jnp
from jax import lax
from jax.experimental import pallas as pl
from jax.experimental.pallas import tpu as pltpu
from jax.sharding import PartitionSpec as P

MESH = pl.DeviceIdType.MESH
F32 = jnp.float32
BF16 = jnp.bfloat16
NT = (((1,), (1,)), ((), ()))
NN = (((1,), (0,)), ((), ()))
HIDDEN = -1e30
LOG2E = 1.4426950408889634

TOKENS = 64
GROUP = 8
WIDTH = 128
ROWS = TOKENS * GROUP
SPAN = 1024
STRIP = 256
HALF = ROWS // 2
RING = 8
FEATURES = GROUP * WIDTH
COLUMNS = 512
SCALE = WIDTH ** -0.5 * LOG2E


def kernel(
    q_ref, k_ref, v_ref, len_ref, plen_ref, w_ref, out_ref,
    q_all, k_all, vt_all, score, peak, acc, top,
    go_o, go_s, in_o, in_s, turn, mixed, part, mate_in, y_out, y_in, own,
    kv_send, kv_recv, q_send, q_recv, rs_send, rs_recv, rt_send, rt_recv,
    mx_send, mx_recv, ag_send, ag_recv, co_send, co_recv, y_send, y_recv,
):
    ctx = lax.axis_index("ctx")
    head = lax.axis_index("head")
    side, z = ctx // RING, ctx % RING
    y, core = head // 2, head % 2

    def z_at(step):
        return {"ctx": side * RING + (z + step + RING) % RING}

    def y_at(to):
        return {"head": to * 2 + core}

    partner = {"ctx": (1 - side) * RING + z}
    mate = {"head": y * 2 + 1 - core}

    def remote(src, dst, send, recv, to):
        return pltpu.make_async_remote_copy(
            src_ref=src, dst_ref=dst, send_sem=send, recv_sem=recv,
            device_id=to, device_id_type=MESH,
        )

    barrier = pltpu.get_barrier_semaphore()
    for to in (z_at(1), z_at(-1), partner, mate, y_at((y + 1) % 4), y_at((y + 2) % 4), y_at((y + 3) % 4)):
        pl.semaphore_signal(barrier, inc=1, device_id=to, device_id_type=MESH)

    plen = plen_ref[0]

    def chunk_start(chunk):
        holder = jnp.where(chunk < 2, side, 1 - side)
        return (holder * RING + z) * 2 * SPAN + (chunk % 2) * SPAN

    q_all[0] = q_ref[...]
    for chunk in range(2):
        start = chunk_start(chunk)
        rows = pl.ds(chunk * SPAN, SPAN)
        keys = k_ref[rows, :].astype(F32)
        seen = start + lax.broadcasted_iota(jnp.int32, (SPAN, WIDTH), 0) < plen
        k_all[chunk] = jnp.where(seen, keys, keys[0:1, :]).astype(BF16)
        vals = jnp.where(seen, v_ref[rows, :].astype(F32), 0.0)
        vt_all[chunk, 0:WIDTH, :] = vals.T.astype(BF16)
    for chunk in range(4):
        seen = chunk_start(chunk) + lax.broadcasted_iota(jnp.int32, (16, SPAN), 1) < plen
        vt_all[chunk, WIDTH:, :] = jnp.where(seen, 1.0, 0.0).astype(BF16)
    acc[...] = jnp.zeros_like(acc)
    top[...] = jnp.full_like(top, HIDDEN)

    def q_copy(n, half, slot):
        to = jnp.where(slot % 2 == 1, 1, -1)
        rows = pl.ds(half * HALF, HALF)
        return remote(
            q_all.at[n, rows], q_all.at[slot, rows],
            q_send.at[slot * 2 + half], q_recv.at[slot * 2 + half], z_at(to),
        )

    def kv_copy(index):
        chunk = index // 2
        if index % 2 == 0:
            src, dst = k_all.at[chunk], k_all.at[chunk + 2]
        else:
            src, dst = vt_all.at[chunk, 0:WIDTH], vt_all.at[chunk + 2, 0:WIDTH]
        return remote(src, dst, kv_send.at[index], kv_recv.at[index], partner)

    pl.semaphore_wait(barrier, 7)
    for half in range(2):
        for slot in (1, 2):
            q_copy(0, half, slot).start()
    for index in range(4):
        kv_copy(index).start()

    def task(t):
        n = jnp.where(t < 16, t // 2, jnp.where(t < 24, t - 16, 31 - t))
        chunk = jnp.where(t < 16, t % 2, jnp.where(t < 24, 2, 3))
        return n, chunk

    def ready(t):
        @pl.when(jnp.logical_and(jnp.logical_and(t >= 2, t < 16), t % 2 == 0))
        def _():
            n = t // 2
            for half in range(2):
                q_copy(0, half, n).wait_recv()

                @pl.when(n + 2 < RING)
                def _():
                    q_copy(n, half, n + 2).start()

        @pl.when(t == 16)
        def _():
            kv_copy(0).wait_recv()
            kv_copy(1).wait_recv()

        @pl.when(t == 24)
        def _():
            kv_copy(2).wait_recv()
            kv_copy(3).wait_recv()

    def step(ahead, slot_ahead, now, slot_now):
        if ahead is not None:
            n_ahead, c_ahead = task(ahead)
            queries = q_all[n_ahead]
        if now is not None:
            n_now, c_now = task(now)
            best = peak[slot_now, 0:1, :]
        total = highest = None
        for strip in range(0, SPAN, STRIP):
            at = pl.ds(strip, STRIP)
            if ahead is not None:
                s = lax.dot_general(k_all[c_ahead, at, :], queries, NT, preferred_element_type=F32)
                score[slot_ahead, at, :] = s
                high = jnp.max(s.reshape(STRIP // 8, 8, ROWS), axis=0)
                highest = high if highest is None else jnp.maximum(highest, high)
            if now is not None:
                weights = jnp.exp2((score[slot_now, at, :] - best) * SCALE).astype(BF16)
                term = lax.dot_general(vt_all[c_now, :, at], weights, NN, preferred_element_type=F32)
                total = term if total is None else total + term
        if ahead is not None:
            peak[slot_ahead, 0:1, :] = jnp.max(highest, axis=0, keepdims=True)
        if now is not None:
            best = jnp.where(chunk_start(c_now) < plen, best, HIDDEN)
            old = top[n_now, 0:1, :]
            new = jnp.maximum(old, best)
            top[n_now, 0:1, :] = new
            acc[n_now] = acc[n_now] * jnp.exp2((old - new) * SCALE) + total[0:136] * jnp.exp2((best - new) * SCALE)

    def rs_copies(n, half):
        to = jnp.where(n % 2 == 1, -1, 1)
        lanes = pl.ds(half * HALF, HALF)
        i = n * 2 + half
        return (
            remote(go_o.at[i], in_o.at[i], rs_send.at[i], rs_recv.at[i], z_at(to)),
            remote(go_s.at[i], in_s.at[i], rt_send.at[i], rt_recv.at[i], z_at(to)),
        )

    def join(n, half, source):
        for copy in rs_copies(source, half):
            copy.wait_recv()
        lanes = pl.ds(half * HALF, HALF)
        i = source * 2 + half
        old, best = top[n, 0:1, lanes], in_s[i, 0:1, :]
        new = jnp.maximum(old, best)
        keep, add = jnp.exp2((old - new) * SCALE), jnp.exp2((best - new) * SCALE)
        top[n, 0:1, lanes] = new
        acc[n, 0:WIDTH, lanes] = acc[n, 0:WIDTH, lanes] * keep + in_o[i].astype(F32) * add
        acc[n, WIDTH:, lanes] = acc[n, WIDTH:, lanes] * keep + in_s[i, 8:16, :] * add

    def pass_on(t):
        n = 31 - t
        for half in range(2):
            lanes = pl.ds(half * HALF, HALF)

            @pl.when(jnp.logical_and(t >= 24, n + 2 < RING))
            def _():
                join(n, half, n + 2)

            @pl.when(jnp.logical_and(t >= 24, n >= 1))
            def _():
                i = n * 2 + half
                go_o[i] = acc[n, 0:WIDTH, lanes].astype(BF16)
                go_s[i, 0:8, :] = top[n, :, lanes]
                go_s[i, 8:16, :] = acc[n, WIDTH:, lanes]
                for copy in rs_copies(n, half):
                    copy.start()

    ready(0)
    step(0, 0, None, None)

    def two(g, _):
        t = g * 2
        ready(t + 1)
        step(t + 1, 1, t, 0)
        pass_on(t)
        ready(t + 2)
        step(jnp.minimum(t + 2, 31), 0, t + 1, 1)
        pass_on(t + 1)
        return 0

    lax.fori_loop(0, 16, two, 0)
    for half in range(2):
        join(0, half, 1)

    token = lax.broadcasted_iota(jnp.int32, (1, ROWS), 1) // GROUP
    live = z * TOKENS + token < jnp.where(side == 0, len_ref[0], len_ref[1])
    done = jnp.where(live, acc[0, 0:WIDTH, :] / acc[0, WIDTH:WIDTH + 1, :], 0.0)
    turn[...] = done.T
    for j in range(GROUP):
        mixed[side, 0, :, j * WIDTH:(j + 1) * WIDTH] = turn[pl.ds(j, TOKENS, stride=GROUP), :].astype(BF16)

    def of_stream(stream):
        return side if stream == 0 else 1 - side

    def ag_copy(stream, n, slot):
        up = 1 if stream == 0 else 0
        to = jnp.where(slot % 2 == up, 1, -1)
        where = of_stream(stream)
        i = stream * RING + slot
        return remote(mixed.at[where, n], mixed.at[where, slot], ag_send.at[i], ag_recv.at[i], z_at(to))

    across = remote(mixed.at[side, 0], mixed.at[side, 0], mx_send, mx_recv, partner)
    across.start()
    for slot in (1, 2):
        ag_copy(0, 0, slot).start()

    def arrive(stream, n):
        ag_copy(stream, 0, n).wait_recv()

        @pl.when(n + 2 < RING)
        def _():
            ag_copy(stream, n, n + 2).start()

    def project(slot_own, slot_other, at):
        slot_0 = jnp.where(side == 0, slot_own, slot_other)
        slot_1 = jnp.where(side == 0, slot_other, slot_own)
        part[at, 0:TOKENS] = jnp.dot(mixed[0, slot_0], w_ref[...], preferred_element_type=F32)
        part[at, TOKENS:] = jnp.dot(mixed[1, slot_1], w_ref[...], preferred_element_type=F32)

        @pl.when((at // 2) % 2 != core)
        def _():
            to_mate(at).start()

    def to_mate(at):
        return remote(part.at[at], mate_in.at[at], co_send.at[at], co_recv.at[at], mate)

    def y_copy(index, to):
        return remote(y_out.at[index], y_in.at[y * 2 + index % 2], y_send.at[index], y_recv.at[y * 2 + index % 2], y_at(to))

    def spread(at):
        @pl.when((at // 2) % 2 == core)
        def _():
            to_mate(at).wait_recv()
            for half in range(2):
                to = half * 2 + at // 4
                index = to * 2 + at % 2
                rows = pl.ds(half * TOKENS, TOKENS)
                both = part[at, rows, :] + mate_in[at, rows, :]

                @pl.when(to == y)
                def _():
                    own[at % 2] = both

                @pl.when(to != y)
                def _():
                    y_out[index] = both.astype(BF16)
                    y_copy(index, to).start()

    across.wait_recv()
    for slot in (1, 2):
        ag_copy(1, 0, slot).start()
    project(0, 0, z)

    def below(d):
        return (z - d + RING) % RING

    def above(d):
        return (z + d) % RING

    def round_(d, _):
        for n in (2 * d - 1, 2 * d):
            for stream in range(2):
                arrive(stream, n)
        project(2 * d - 1, 2 * d, below(d))
        project(2 * d, 2 * d - 1, above(d))

        @pl.when(d == 1)
        def _():
            spread(z)

        @pl.when(d > 1)
        def _():
            spread(below(d - 1))
            spread(above(d - 1))

        return 0

    lax.fori_loop(1, 4, round_, 0)
    arrive(0, 7)
    arrive(1, 7)
    project(7, 7, above(4))
    spread(below(3))
    spread(above(3))
    spread(above(4))

    for which in range(2):
        total = own[which]
        for step_ in range(1, 4):
            source = (y + step_) % 4
            y_in_copy = remote(
                y_out.at[which], y_in.at[source * 2 + which], y_send.at[which], y_recv.at[source * 2 + which], y_at(source)
            )
            y_in_copy.wait_recv()
            total = total + y_in[source * 2 + which].astype(F32)
        out_ref[which * TOKENS:(which + 1) * TOKENS, :] = total

    for index in range(4):
        kv_copy(index).wait_send()

    def sent(slot, _):
        for half in range(2):
            q_copy(0, half, slot).wait_send()
            for copy in rs_copies(slot, half):
                copy.wait_send()
        for stream in range(2):
            ag_copy(stream, 0, slot).wait_send()
        return 0

    lax.fori_loop(1, RING, sent, 0)
    across.wait_send()

    def sent_at(at, _):
        @pl.when((at // 2) % 2 != core)
        def _():
            to_mate(at).wait_send()

        @pl.when(at // 2 != y)
        def _():
            y_copy(at, at // 2).wait_send()

        return 0

    lax.fori_loop(0, RING, sent_at, 0)


def body(queries, keys, values, lengths, prompt_lengths, out_weight):
    vmem = pl.BlockSpec(memory_space=pltpu.VMEM)
    smem = pl.BlockSpec(memory_space=pltpu.SMEM)
    dma = pltpu.SemaphoreType.DMA
    return pl.pallas_call(
        kernel,
        out_shape=jax.ShapeDtypeStruct((2 * TOKENS, COLUMNS), F32),
        in_specs=[vmem, vmem, vmem, smem, smem, vmem],
        out_specs=vmem,
        scratch_shapes=[
            pltpu.VMEM((RING, ROWS, WIDTH), BF16),
            pltpu.VMEM((4, SPAN, WIDTH), BF16),
            pltpu.VMEM((4, WIDTH + 16, SPAN), BF16),
            pltpu.VMEM((2, SPAN, ROWS), F32),
            pltpu.VMEM((2, 8, ROWS), F32),
            pltpu.VMEM((RING, WIDTH + 8, ROWS), F32),
            pltpu.VMEM((RING, 8, ROWS), F32),
            pltpu.VMEM((2 * RING, WIDTH, HALF), BF16),
            pltpu.VMEM((2 * RING, 16, HALF), F32),
            pltpu.VMEM((2 * RING, WIDTH, HALF), BF16),
            pltpu.VMEM((2 * RING, 16, HALF), F32),
            pltpu.VMEM((ROWS, WIDTH), F32),
            pltpu.VMEM((2, RING, TOKENS, FEATURES), BF16),
            pltpu.VMEM((RING, 2 * TOKENS, COLUMNS), F32),
            pltpu.VMEM((RING, 2 * TOKENS, COLUMNS), F32),
            pltpu.VMEM((8, TOKENS, COLUMNS), BF16),
            pltpu.VMEM((8, TOKENS, COLUMNS), BF16),
            pltpu.VMEM((2, TOKENS, COLUMNS), F32),
            dma((4,)), dma((4,)),
            dma((2 * RING,)), dma((2 * RING,)),
            dma((2 * RING,)), dma((2 * RING,)),
            dma((2 * RING,)), dma((2 * RING,)),
            dma, dma,
            dma((2 * RING,)), dma((2 * RING,)),
            dma((RING,)), dma((RING,)),
            dma((8,)), dma((8,)),
        ],
        compiler_params=pltpu.CompilerParams(
            collective_id=1, has_side_effects=True, vmem_limit_bytes=48 << 20
        ),
        name="paired_attention",
    )(
        queries.reshape(ROWS, WIDTH),
        keys.reshape(2 * SPAN, WIDTH),
        values.reshape(2 * SPAN, WIDTH),
        lengths,
        prompt_lengths,
        out_weight,
    )


def solution(mesh):
    in_specs = (
        P(("pair", "ctx"), "head", None),
        P(("pair", "ctx"), "head", None),
        P(("pair", "ctx"), "head", None),
        P("pair"),
        P("pair"),
        P("head", "ctx"),
    )
    out_specs = P(("pair", "head"), "ctx")
    return jax.shard_map(body, mesh=mesh, in_specs=in_specs, out_specs=out_specs, check_vma=False)
```

time: 425 us -> 93.6 us (0.22)
  the two profiles are of different devices: /device:TPU:7 before, /device:TPU:1 now
where the time goes in v1:
time: 93.6 us; the launch traced here: 93.4 us
  Pallas kernels  87.1 us (93%)
  local copies, waits for them, and re-layouts  5.56 us (6%)
    pallas_call x1, Pallas kernels, body(): pl.pallas_call(kernel, out_shape=jax.ShapeDtypeStruct((2 * TOKENS, COLUMN...  87.1 us
    unnamed x11, local copies, waits for them, and re-layouts  5.56 us

profile of v1, /device:TPU:1, one launch (start us, length us, event | category | flops | bytes accessed | tf_op | source)
XLA Modules:
  0.0 93.4 jit_solution(13053897588202428489)
XLA Ops:
  0.7 0.0 copy-start.4
  0.7 0.6 copy-done.4
  1.3 0.0 copy-start
  1.3 1.2 %copy-done = bf16[1024,512]{1,0:T(8,128)(2,1)S(1)} copy-done((bf16[1024,512]{1,0:T(8,128)(2,1)S(1)}, bf16[1024,512]{1,0:T(8,128)(2,1)}, u32[]{:S(2)}) %copy-start) | copy-done | bytes 1048600
  2.5 0.0 copy-start.1
  2.5 1.0 %copy-done.1 = bf16[2048,1,128]{2,0,1:T(8,128)(2,1)S(1)} copy-done((bf16[2048,1,128]{2,0,1:T(8,128)(2,1)S(1)}, bf16[2048,1,128]{2,0,1:T(8,128)(2,1)}, u32[]{:S(2)}) %copy-start.1) | copy-done | bytes 524312
  3.6 0.0 copy-start.2
  3.6 1.0 %copy-done.2 = bf16[2048,1,128]{2,0,1:T(8,128)(2,1)S(1)} copy-done((bf16[2048,1,128]{2,0,1:T(8,128)(2,1)S(1)}, bf16[2048,1,128]{2,0,1:T(8,128)(2,1)}, u32[]{:S(2)}) %copy-start.2) | copy-done | bytes 524312
  4.6 0.0 copy-start.3
  4.6 0.9 copy-done.3
  5.5 87.1 %paired_attention.1 = f32[128,512]{1,0:T(8,128)S(1)} custom-call(bf16[512,128]{1,0:T(8,128)(2,1)S(1)} %bitcast.5, bf16[2048,128]{1,0:T(8,128)(2,1)S(1)} %bitcast.3, bf16[2048,128]{1,0:T(8,128)(2,1)S(1)} %bitcast.4, s32[2]{0:T(128)S(1)} %copy-done.4, s32[1]{0:T(128)S(6)} %copy.8.plen_ref, bf16[1024,512]{1,0:T(8,128)(2,1)S(1)} %copy-done), custom_call_target="tpu_custom_call" | custom-call | tf_op jit(solution)/shard_map/paired_attention/pallas_call | solution.py:361
  92.7 0.7 copy.9
Async XLA Ops:
  0.7 0.7 copy-start.4
  1.3 1.2 %copy-start = (bf16[1024,512]{1,0:T(8,128)(2,1)S(1)}, bf16[1024,512]{1,0:T(8,128)(2,1)}, u32[]{:S(2)}) copy-start(bf16[1024,512]{1,0:T(8,128)(2,1)} %w_ref.1) | copy-start | bytes 3145732
  2.5 1.0 %copy-start.1 = (bf16[2048,1,128]{2,0,1:T(8,128)(2,1)S(1)}, bf16[2048,1,128]{2,0,1:T(8,128)(2,1)}, u32[]{:S(2)}) copy-start(bf16[2048,1,128]{2,0,1:T(8,128)(2,1)} %param.7) | copy-start | bytes 1572868
  3.6 1.0 %copy-start.2 = (bf16[2048,1,128]{2,0,1:T(8,128)(2,1)S(1)}, bf16[2048,1,128]{2,0,1:T(8,128)(2,1)}, u32[]{:S(2)}) copy-start(bf16[2048,1,128]{2,0,1:T(8,128)(2,1)} %param.8) | copy-start | bytes 1572868
  4.6 0.9 copy-start.3
